TPU v7x, 32 devices: a whole 2x2x4 slice. The times are simulated.
32 devices in a mesh: spot: 16 (over z, y, x), gene: 2 (over core).
Axes of the slice: x: 2, y: 2, z: 4, core: 2. Of those that a mesh axis runs over, the one named last changes fastest.
Arguments:
- logits: float32 [2, 1024, 2048], P(None, 'spot'), may hold values from -12 to 12
- expr: float32 [2048, 2048], P('spot', 'gene'), may hold values from -6 to 6
- spatial: float32 [2, 1024, 2048], P(None, 'spot', 'gene')
- slide_spots: int32 [2], replicated, may hold values from 768 to 1024, as said below
- spot_cells: int32 [2, 1024], P(None, 'spot'), may hold values from 1 to 20
- cell_prior: int32 [2048], replicated, may hold values from 4096 to 262143
Outputs:
- pred: float32 [2, 1024, 2048], P(None, 'spot', 'gene')
- loss: float32 [], replicated
- grad_logits: float32 [2, 1024, 2048], P(None, 'spot')
- grad_expr: float32 [2048, 2048], P('spot', 'gene')
Inputs may be any that keep to these rules, and one draw needn't show every extreme that they name: `slide_spots`: one slide, drawn from the seed, fills all 1024 slots in every draw; every other slide leaves at least one slot empty.
All inputs are finite; a program needn't handle non-finite values.
Results may differ from a plain program's by a relative error of at most 0.0003.
Values sent between devices are 32-bit elements; how exact they have to be, the bound alone decides.
A program may use at most 192 MiB of HBM per device.

v0:
```python
import functools

import jax
import jax.numpy as jnp
from jax import lax
from jax.experimental import pallas as pl
from jax.experimental.pallas import tpu as pltpu
from jax.sharding import PartitionSpec as P

tiny = 1e-06
fixed_point = 16384.0
F32 = jnp.float32
BF16 = jnp.bfloat16
MESH = pl.DeviceIdType.MESH

PLANE = 4
LANES = 128
STEP_ROWS = 16
BLOCK = 32
TALL = 256
FORWARD = (128, 256, 256, 128, 128, 128)
BACKWARD = (128, 128, 256, 256, 256)
SPLIT = 4
LEAD = 1
NEAR_LEAD = 3
EARLY = 3
STEPS = (
    ("far", 0),
    ("far", 1),
    ("near", 0),
    ("share",),
    ("far", 2),
    ("far", 3),
    ("take",),
    ("whole", 0),
    ("near", 1),
    ("product", 0),
    ("sum", 0),
    ("whole", 1),
    ("near", 2),
    ("product", 1),
    ("whole", 2),
    ("product", 2),
    ("whole", 3),
    ("near", 3),
    ("product", 3),
    ("far", 4),
    ("whole", 4),
    ("near", 4),
    ("product", 4),
    ("sum", 1),
    ("turn", 0),
    ("far", 5),
    ("whole", 5),
    ("near", 5),
    ("product", 5),
    ("sum", 2),
    ("plane", 0),
    ("turn", 1),
    ("sum", 3),
    ("line", 0),
    ("sum", 4),
    ("sum", 5),
    ("plane", 1),
    ("cores",),
    ("genes", 0),
    ("spots",),
    ("grad", 0),
    ("grad", 1),
    ("grad", 2),
    ("line", 1),
    ("backward", 0),
    ("backward", 1),
    ("add_near", 0),
    ("genes", 1),
    ("grad", 3),
    ("backward", 2),
    ("probs", 0),
    ("add_far", 0),
    ("probs", 1),
    ("expr", 0),
    ("grad", 4),
    ("add_near", 1),
    ("probs", 2),
    ("terms",),
    ("backward", 3),
    ("probs", 3),
    ("add_near", 2),
    ("backward", 4),
    ("add_far", 1),
    ("probs", 4),
    ("exchange",),
    ("add_near", 3),
    ("add_far", 2),
    ("left",),
    ("return",),
    ("loss",),
    ("add_far", 3),
    ("expr", 1),
    ("add_near", 4),
    ("logits",),
    ("add_far", 4),
    ("expr", 2),
    ("expr", 3),
    ("expr", 4),
)


def halves(value):
    high = value.astype(BF16)
    return high, (value - high.astype(F32)).astype(BF16)


def threefold(value):
    high, low = halves(value)
    return jnp.concatenate([high, high, low], axis=1)


def product(a, b, contract):
    return lax.dot_general(a, b, (contract, ((), ())), preferred_element_type=F32)


def plane_kernel(lines, forward_widths, backward_widths, *refs):
    chunks, turns = len(forward_widths), len(backward_widths)
    (
        (logits_ref, expr_ref, spatial_ref, count_in, cells_in, prior_in),
        (pr, loss_ref, glog, ge),
        (count_ref, cells_ref, prior_ref, lg, lq, tg, ex, pq, ab, af, probs_3, turned_3, expr_3, sacc, s1, s2, gv, ss, rowv, rs),
        (grad_3, factor, t0, p0, vr, fs, fx, fy, fz, fr, inn, l1, l2),
        (loc, ou_s, ou_r, od_s, od_r, fu_s, fu_r, fd_s, fd_r, a_s, a_r, a2_s, a2_r, r_s, r_r),
        (c_s, c_r, s1_s, s1_r, s2_s, s2_r, ss_s, ss_r, d_s, d_r, ru_s, ru_r, rd_s, rd_r),
        (f_s, f_r, fx_s, fx_r, go_s, go_r, in_s, in_r, l1_s, l1_r, l2_s, l2_r, t0_s, t0_r, p0_s, p0_r, vr_s, vr_r),
        bb,
        cs,
        cr,
        ds,
        es,
        ru,
        rd,
    ) = grouped(refs, (6, 4, 20, 13, 15, 14, 18, chunks, chunks, chunks, turns, turns, turns, turns))
    place = lax.axis_index("spot")
    core = lax.axis_index("gene")
    z = place // PLANE
    q = place % PLANE
    col, row = q % 2, q // 2
    mates = ((1 - row) * 2 + 1 - col, row * 2 + 1 - col, (1 - row) * 2 + col)
    others = tuple((z + step) % lines for step in range(1, lines))
    up, down = (place + PLANE, core), (place - PLANE, core)
    sibling = (place, 1 - core)
    slides, slide_rows = logits_ref.shape[0], logits_ref.shape[1]
    rows = slides * slide_rows
    cb = expr_ref.shape[0]
    genes = expr_ref.shape[1]
    last = lines - 1

    def mate(p):
        return (z * PLANE + p, core)

    def send(src, dst, send_sem, recv_sem, device):
        copy = pltpu.make_async_remote_copy(
            src_ref=src, dst_ref=dst, send_sem=send_sem, recv_sem=recv_sem, device_id=device, device_id_type=MESH
        )
        copy.start()

    def arrived(dst, recv_sem):
        pltpu.make_async_copy(dst, dst, recv_sem).wait()

    sent = arrived

    def cols(k):
        return pl.ds(sum(forward_widths[:k]), forward_widths[k])

    def turn_cols(k):
        return pl.ds(sum(backward_widths[:k]), backward_widths[k])

    def block(index):
        return pl.ds(pl.multiple_of(index * cb, cb), cb)

    def share(index):
        return pl.ds(pl.multiple_of(index * rows, rows), rows)

    def half(index):
        return pl.ds(pl.multiple_of(index * slide_rows, slide_rows), slide_rows)

    small = ((prior_in, prior_ref), (count_in, count_ref), (cells_in, cells_ref))
    pltpu.make_async_copy(expr_ref, ex, loc.at[2 * slides]).start()
    for m in range(slides):
        pltpu.make_async_copy(logits_ref.at[m], lg.at[half(m)], loc.at[m]).start()
    for at, (src, dst) in enumerate(small):
        pltpu.make_async_copy(src, dst, loc.at[2 * slides + 1 + at]).start()
    for m in range(slides):
        pltpu.make_async_copy(spatial_ref.at[m], tg.at[half(m)], loc.at[slides + m]).start()

    barrier = pltpu.get_barrier_semaphore()
    for p in mates:
        pl.semaphore_signal(barrier, inc=1, device_id=mate(p), device_id_type=MESH)
    for o in others:
        pl.semaphore_signal(barrier, inc=1, device_id=(o * PLANE + q, core), device_id_type=MESH)
    pl.semaphore_signal(barrier, inc=1, device_id=sibling, device_id_type=MESH)
    pltpu.make_async_copy(expr_ref, ex, loc.at[2 * slides]).wait()
    for k in range(chunks):
        bb[k][block(z), :] = ex[:, cols(k)]
    for m in range(slides):
        pltpu.make_async_copy(logits_ref.at[m], lg.at[half(m)], loc.at[m]).wait()
    for p in range(PLANE):
        for line in range(lines):
            lq[p, :, pl.ds(line * cb, cb)] = lg[half(core), pl.ds((line * PLANE + p) * cb, cb)]
    pl.semaphore_wait(barrier, len(mates) + len(others) + 1)

    def own_up(k):
        here = bb[k].at[block(z)]
        send(here, here, ou_s.at[k], ou_r.at[k], up)

    def own_down(k):
        here = bb[k].at[block(z)]
        send(here, here, od_s.at[k], od_r.at[k], down)

    def low(at):
        return 2 * at < lines

    for at in range(lines):

        @pl.when(z == at)
        def _():
            for k in range(chunks):
                if at < last and (at == 0 or k < (LEAD if low(at) else NEAR_LEAD)):
                    own_up(k)
                if at > 0 and (at == last or k < (NEAR_LEAD if low(at) else LEAD)):
                    own_down(k)

    for p in mates:
        send(lq.at[p], ab.at[q, half(core)], a_s, a_r.at[q], mate(p))

    def from_below(k, at):
        arrived(bb[k].at[pl.ds((at - 1) * cb, cb)], ou_r.at[k])
        if at > 1:
            arrived(bb[k].at[pl.ds(0, (at - 1) * cb)], fu_r.at[k])

    def from_above(k, at):
        arrived(bb[k].at[pl.ds((at + 1) * cb, cb)], od_r.at[k])
        if at < last - 1:
            arrived(bb[k].at[pl.ds((at + 2) * cb, (last - 1 - at) * cb)], fd_r.at[k])

    def upward(k, at):
        from_below(k, at)
        here = bb[k].at[pl.ds(0, at * cb)]
        send(here, here, fu_s.at[k], fu_r.at[k], up)

    def downward(k, at):
        from_above(k, at)
        here = bb[k].at[pl.ds((at + 1) * cb, (last - at) * cb)]
        send(here, here, fd_s.at[k], fd_r.at[k], down)

    def forward_far(k):
        for at in range(1, last):

            @pl.when(z == at)
            def _():
                (upward if low(at) else downward)(k, at)
                if k + LEAD < chunks:
                    (own_up if low(at) else own_down)(k + LEAD)

    def forward_near(k):
        for at in range(1, last):

            @pl.when(z == at)
            def _():
                (downward if low(at) else upward)(k, at)
                if k + NEAR_LEAD < chunks:
                    (own_down if low(at) else own_up)(k + NEAR_LEAD)

    def gathered(k):
        @pl.when(z == 0)
        def _():
            from_above(k, 0)

        @pl.when(z == last)
        def _():
            from_below(k, last)

    for at, (src, dst) in enumerate(small):
        pltpu.make_async_copy(src, dst, loc.at[2 * slides + 1 + at]).wait()
    weights = prior_ref[...].astype(F32) / fixed_point

    @pl.loop(0, rows // STEP_ROWS)
    def _(step):
        at = pl.ds(pl.multiple_of(step * STEP_ROWS, STEP_ROWS), STEP_ROWS)
        value = lg[at, :]
        peak = jnp.max(value, axis=1, keepdims=True)
        raised = jnp.exp(value - peak)
        scale = 1.0 / jnp.sum(raised, axis=1, keepdims=True)
        probs = raised * scale
        mass_rows = jnp.sum(probs * weights, axis=1, keepdims=True)
        rowv[0, at, :] = jnp.broadcast_to(mass_rows, (STEP_ROWS, LANES))
        rowv[1, at, :] = jnp.broadcast_to(peak, (STEP_ROWS, LANES))
        rowv[2, at, :] = jnp.broadcast_to(scale, (STEP_ROWS, LANES))
        for p in range(PLANE):
            for line in range(lines):
                at_cells = (line * PLANE + p) * cb
                pq[p, at, pl.ds(line * cb, cb)] = probs[:, at_cells : at_cells + cb]

    wide = lax.broadcasted_iota(jnp.int32, (rows, LANES), 1)
    rs[q] = jnp.where(wide == 0, rowv[1], rowv[2]).T[0:8]
    for p in mates:
        send(rs.at[q], rs.at[q], r_s, r_r.at[q], mate(p))

    rid = lax.broadcasted_iota(jnp.int32, (rows, 1), 0)
    first = rid < slide_rows
    position = place * slide_rows + jnp.where(first, rid, rid - slide_rows)
    count = jnp.where(first, count_ref[0], count_ref[1])
    valid = (position < count).astype(F32)
    scale_count = count.astype(F32)
    square = (slide_rows, slide_rows)
    eye = lax.broadcasted_iota(jnp.int32, square, 0) == lax.broadcasted_iota(jnp.int32, square, 1)
    counted = jnp.concatenate(
        [
            jnp.sum(jnp.where(eye, cells_ref[m : m + 1, :].astype(F32), 0.0), axis=1, keepdims=True)
            for m in range(slides)
        ],
        axis=0,
    )
    mass = rowv[0, :, 0:1]
    kcell = valid * counted

    def by_slide(value):
        return [jnp.sum(value[m * slide_rows : (m + 1) * slide_rows], axis=0, keepdims=True) for m in range(slides)]

    mass_parts = by_slide(valid * mass)
    cell_parts = by_slide(kcell)
    lane = lax.broadcasted_iota(jnp.int32, (1, LANES), 1)
    scalars = jnp.zeros((1, LANES), F32)
    for at, value in enumerate(mass_parts + cell_parts):
        scalars = jnp.where(lane == at, value, scalars)
    for m in range(slides):
        pltpu.make_async_copy(spatial_ref.at[m], tg.at[half(m)], loc.at[slides + m]).wait()

    head = backward_widths[0]
    t0[q] = tg[:, 0:head]
    for p in mates:
        send(t0.at[q], t0.at[q], t0_s, t0_r.at[q], mate(p))
    sacc[...] = jnp.zeros_like(sacc)
    s1[q, 3 * slides :, :] = jnp.zeros((8 - 3 * slides, genes), F32)
    s1[q, 3 * slides : 3 * slides + 1, 0:LANES] = scalars

    def share_logits():
        for p in (mates[1], mates[2], mates[0]):
            here = ab.at[p, half(core)]
            arrived(here, a_r.at[p])
            send(here, here, a2_s, a2_r.at[p], sibling)

    def lay_probs(p, at, value):
        af[p, at, :] = value
        there = pl.ds(pl.multiple_of(p * rows + at.start, BLOCK), BLOCK)
        probs_3[there, :] = threefold(value)

    def take_probs():
        in_blocks(0, rows, lambda at: lay_probs(q, at, pq[q, at, :]))
        for p in (mates[1], mates[2], mates[0]):
            arrived(rs.at[p], r_r.at[p])
            arrived(ab.at[p, half(1 - core)], a2_r.at[p])
            rowv[1] = jnp.concatenate([rs[p].T, jnp.zeros((rows, LANES - 8), F32)], axis=1)

            def take(at):
                probs = jnp.exp(ab[p, at, :] - rowv[1, at, 0:1]) * rowv[1, at, 1:2]
                lay_probs(p, at, probs)

            in_blocks(0, rows, take)

    def transpose(part):
        @pl.loop(0, PLANE // 2)
        def _(step):
            p = part * (PLANE // 2) + step
            high, low_part = halves(af[p].T)
            for third, value in enumerate((high, high, low_part)):
                turned_3[:, pl.ds(pl.multiple_of(third * PLANE * rows + p * rows, rows), rows)] = value

    def in_blocks(start, count, body):
        @pl.loop(0, count // BLOCK)
        def _(step):
            body(pl.ds(pl.multiple_of(start + step * BLOCK, BLOCK), BLOCK))

    quarter = lines * cb

    def lay_factor(at, length, width, value):
        high, low_part = halves(value)
        for third, part in enumerate((high, low_part, high)):
            here = pl.ds(pl.multiple_of(third * length + at.start, BLOCK), BLOCK)
            factor[here, 0:width] = part

    def keep_expr(k, at, value):
        start = sum(forward_widths[:k])
        for turn in range(turns):
            origin, width = sum(backward_widths[:turn]), backward_widths[turn]
            lo, hi = max(start, origin), min(start + forward_widths[k], origin + width)
            if lo < hi:
                high, low_part = halves(value[:, lo - start : hi - start])
                for third, part in enumerate((high, low_part, high)):
                    expr_3[at, pl.ds(3 * origin + third * width + lo - origin, hi - lo)] = part

    def three_turn_cols(k):
        return pl.ds(3 * sum(backward_widths[:k]), 3 * backward_widths[k])

    def forward_product(k):
        width = forward_widths[k]

        def lay(at):
            value = bb[k][at, :]
            lay_factor(at, quarter, width, value)
            keep_expr(k, at, value)

        in_blocks(0, quarter, lay)
        if k < chunks - 1:

            @pl.loop(0, PLANE * rows // TALL)
            def _(step):
                tall = pl.ds(pl.multiple_of(step * TALL, TALL), TALL)
                cs[k][tall, :] = product(probs_3[tall, :], factor[0 : 3 * quarter, 0:width], ((1,), (0,)))

            for p in mates:
                pass_pred(k, p)
        else:
            for side, served in ((1 - row, (mates[0], mates[2])), (row, (mates[1],))):
                pair = pl.ds(pl.multiple_of(2 * side * rows, 2 * rows), 2 * rows)
                cs[k][pair, :] = product(probs_3[pair, :], factor[0 : 3 * quarter, 0:width], ((1,), (0,)))
                for p in served:
                    pass_pred(k, p)

    def pass_pred(k, p):
        send(cs[k].at[share(p)], cr[k].at[q], c_s.at[k], c_r.at[k, q], mate(p))

    def finish_pred(k):
        total = cs[k][share(q), :]
        for p in mates:
            arrived(cr[k].at[p], c_r.at[k, p])
            total = total + cr[k][p]
        pr[:, cols(k)] = total
        if k == 0:
            p0[q] = total[:, 0:head]
            for p in mates:
                send(p0.at[q], p0.at[q], p0_s, p0_r.at[q], mate(p))
        truth = tg[:, cols(k)]
        for at, value in enumerate((total * truth, total * total, truth * truth)):
            sacc[at] += lane_groups(value)
        kept = valid * total
        stats = by_slide(kept * truth) + by_slide(kept * total) + by_slide(valid * truth * truth)
        s1[q, 0 : 3 * slides, cols(k)] = jnp.concatenate(stats, axis=0)

    early = sum(forward_widths[:EARLY])
    parts = (pl.ds(0, early), pl.ds(early, genes - early))

    def sum_plane(at):
        for p in mates:
            send(s1.at[q, :, parts[at]], s1.at[q, :, parts[at]], s1_s, s1_r.at[at, q], mate(p))

    def sum_line(at):
        for p in mates:
            arrived(s1.at[p, :, parts[at]], s1_r.at[at, p])
        s2[z, :, parts[at]] = (s1[0, :, parts[at]] + s1[1, :, parts[at]]) + (s1[2, :, parts[at]] + s1[3, :, parts[at]])
        for o in others:
            send(s2.at[z, :, parts[at]], s2.at[z, :, parts[at]], s2_s, s2_r.at[at, z], (o * PLANE + q, core))

    kept = {}

    def finish_genes(at):
        for o in others:
            arrived(s2.at[o, :, parts[at]], s2_r.at[at, o])
        total = s2[0, :, parts[at]]
        for line in range(1, lines):
            total = total + s2[line, :, parts[at]]
        gene_dot, gene_pred, gene_true = total[0:2], total[2:4], total[4:6]
        gene_inv = lax.rsqrt(gene_pred * gene_true + tiny)
        cos_gene = gene_dot * gene_inv
        gv[0:2, parts[at]] = gene_inv
        gv[2:4, parts[at]] = cos_gene * gene_true / (gene_pred * gene_true + tiny)
        kept["genes", at] = jnp.sum(jnp.sum(cos_gene, axis=1, keepdims=True), axis=0, keepdims=True)
        if at == 0:
            kept["mass"] = jnp.where(first, total[6:7, 0:1], total[6:7, 1:2])
            kept["cells"] = jnp.where(first, total[6:7, 2:3], total[6:7, 3:4])

    def sum_cores():
        sums = [jnp.sum(sacc[at], axis=1, keepdims=True) for at in range(3)]
        ss[core] = jnp.where(wide == 0, sums[0], jnp.where(wide == 1, sums[1], sums[2])).T[0:8]
        send(ss.at[core], ss.at[core], ss_s, ss_r, sibling)

    def finish_spots():
        lane_id = lax.broadcasted_iota(jnp.int32, (1, rows), 1)
        first_lane = lane_id < slide_rows
        lane_position = place * slide_rows + jnp.where(first_lane, lane_id, lane_id - slide_rows)
        lane_valid = (lane_position < jnp.where(first_lane, count_ref[0], count_ref[1])).astype(F32)
        arrived(ss.at[1 - core], ss_r)
        spot = ss[0] + ss[1]
        spot_dot, spot_pred, spot_true = spot[0:1], spot[1:2], spot[2:3]
        spot_inv = lax.rsqrt(spot_pred * spot_true + tiny)
        cos_spot = spot_dot * spot_inv
        spot_back = cos_spot * spot_true / (spot_pred * spot_true + tiny)
        kept["cos"] = jnp.sum(lane_valid * cos_spot, axis=1, keepdims=True)
        vectors = [lane_valid * spot_inv, lane_valid * spot_back, lane_valid, jnp.zeros((5, rows), F32)]
        vr[q] = jnp.concatenate(vectors, axis=0)
        sacc[0] = jnp.zeros_like(sacc[0])

    def gradient(truth, guess, by_row, k):
        pieces = []
        for m in range(slides):
            lo, hi = m * slide_rows, (m + 1) * slide_rows
            inverse, back = gv[m : m + 1, turn_cols(k)], gv[2 + m : 3 + m, turn_cols(k)]
            spot_inv, spot_back, spot_valid = by_row[lo:hi, 0:1], by_row[lo:hi, 1:2], by_row[lo:hi, 2:3]
            pieces.append(
                guess[lo:hi] * (spot_valid * back + spot_back) - truth[lo:hi] * (spot_valid * inverse + spot_inv)
            )
        return jnp.concatenate(pieces, axis=0)

    def head_gradient():
        for p in mates:
            arrived(t0.at[p], t0_r.at[p])
            arrived(p0.at[p], p0_r.at[p])
            arrived(vr.at[p], vr_r.at[p])
        for p in range(PLANE):
            ds[0][share(p), :] = gradient(t0[p], p0[p], vr[p].T, 0)
        sacc[0] += lane_groups(ds[0][share(q), :] * p0[q])

    def send_grad(k):
        if k == 0:
            for p in mates:
                send(vr.at[q], vr.at[q], vr_s, vr_r.at[q], mate(p))
            kept["by_row"] = vr[q].T
            return
        grad = gradient(tg[:, turn_cols(k)], pr[:, turn_cols(k)], kept["by_row"], k)
        here = ds[k].at[share(q)]
        here[...] = grad
        for p in mates:
            send(here, here, d_s.at[k], d_r.at[k, q], mate(p))
        sacc[0] += lane_groups(grad * pr[:, turn_cols(k)])

    def send_terms():
        mass_total, cell_total = kept["mass"], kept["cells"]
        portion = kcell / cell_total
        kl_rows = portion * (jnp.log(counted) - jnp.log(cell_total) - jnp.log(mass) + jnp.log(mass_total))
        dmass = scale_count * valid * (1.0 / mass_total - portion / mass)
        terms = jnp.sum(scale_count * kl_rows, axis=0, keepdims=True) - kept["cos"]
        l1[q] = jnp.broadcast_to(terms, (8, LANES))
        for p in mates:
            send(l1.at[q], l1.at[q], l1_s, l1_r.at[q], mate(p))
        inner = jnp.sum(sacc[0], axis=1, keepdims=True)
        inn[core] = jnp.where(wide == 0, inner, kept["genes", 0] + kept["genes", 1])
        send(inn.at[core], inn.at[core], in_s, in_r, sibling)
        rowv[1] = jnp.broadcast_to(dmass, (rows, LANES))

    middle = lines // 2

    def backward_product(k):
        if k == 0:
            head_gradient()
        else:
            for p in mates:
                arrived(ds[k].at[share(p)], d_r.at[k, p])
        width, spots = backward_widths[k], PLANE * rows

        def lay(at):
            value = ds[k][at, :]
            lay_factor(at, spots, width, value)
            grad_3[at, three_turn_cols(k)] = threefold(value)

        in_blocks(0, spots, lay)
        if not halved(k):

            @pl.loop(0, quarter // TALL)
            def _(step):
                tall = pl.ds(pl.multiple_of(step * TALL, TALL), TALL)
                es[k][tall, :] = product(turned_3[tall, :], factor[0 : 3 * spots, 0:width], ((1,), (0,)))

        for turn in range(2):
            if halved(k):
                side = (1 - z // middle) if turn == 0 else z // middle
                pair = pl.ds(pl.multiple_of(side * middle * cb, middle * cb), middle * cb)
                es[k][pair, :] = product(turned_3[pair, :], factor[0 : 3 * spots, 0:width], ((1,), (0,)))

            @pl.when(z == 0)
            def _():
                if halved(k):
                    pass_up(k, middle if turn == 0 else 1, middle if turn == 0 else middle - 1, turn)
                elif whole(k):
                    if turn == 0:
                        pass_up(k, 1, last, 0)
                elif turn == 0:
                    for line in range(last, 0, -1):
                        pass_up(k, line, 1, line)

            @pl.when(z == last)
            def _():
                if halved(k):
                    pass_down(k, 0 if turn == 0 else middle, middle if turn == 0 else middle - 1, turn)
                elif whole(k):
                    if turn == 0:
                        pass_down(k, 0, last, 0)
                elif turn == 0:
                    for line in range(last):
                        pass_down(k, line, 1, line)

    def halved(k):
        return k == 0

    def whole(k):
        return 0 < k < turns - SPLIT

    def pass_up(k, line, count, slot):
        here = pl.ds(line * cb, count * cb)
        send(es[k].at[here], ru[k].at[here], ru_s.at[k], ru_r.at[k, slot], up)

    def pass_down(k, line, count, slot):
        here = pl.ds(line * cb, count * cb)
        send(es[k].at[here], rd[k].at[here], rd_s.at[k], rd_r.at[k, slot], down)

    def take_up(k, line, count, slot):
        arrived(ru[k].at[pl.ds(line * cb, count * cb)], ru_r.at[k, slot])

    def take_down(k, line, count, slot):
        arrived(rd[k].at[pl.ds(line * cb, count * cb)], rd_r.at[k, slot])

    def add_up(k, line, count):
        def add(at):
            es[k][at, :] += ru[k][at, :]

        in_blocks(line * cb, count * cb, add)

    def add_down(k, line, count):
        def add(at):
            es[k][at, :] += rd[k][at, :]

        in_blocks(line * cb, count * cb, add)

    def rising(k, at):
        if halved(k) or whole(k):
            start = middle if halved(k) else at
            take_up(k, start, lines - start, 0)
            above = max(at + 1, start)
            add_up(k, above, lines - above)
            pass_up(k, above, lines - above, 0)
        else:
            for line in range(last, at, -1):
                take_up(k, line, 1, line)
                add_up(k, line, 1)
                pass_up(k, line, 1, line)

    def falling(k, at):
        if halved(k) or whole(k):
            end = middle if halved(k) else at + 1
            take_down(k, 0, end, 0)
            below = min(at, end)
            add_down(k, 0, below)
            pass_down(k, 0, below, 0)
        else:
            for line in range(at):
                take_down(k, line, 1, line)
                add_down(k, line, 1)
                pass_down(k, line, 1, line)

    def add_near(k):
        for at in range(1, last):

            @pl.when(z == at)
            def _():
                (rising if low(at) else falling)(k, at)

    def add_far(k):
        for at in range(1, last):

            @pl.when(z == at)
            def _():
                (falling if low(at) else rising)(k, at)

    def finish_expr(k):
        for at in range(lines):

            @pl.when(z == at)
            def _():
                if at > 0:
                    if halved(k) and at < middle:
                        take_up(k, at, 1, 1)
                    elif at == last and (halved(k) or whole(k)):
                        take_up(k, at, 1, 0)
                    elif not halved(k) and not whole(k):
                        take_up(k, at, 1, at)
                if at < last:
                    if halved(k) and at >= middle:
                        take_down(k, at, 1, 1)
                    elif at == 0 and (halved(k) or whole(k)):
                        take_down(k, at, 1, 0)
                    elif not halved(k) and not whole(k):
                        take_down(k, at, 1, at)

        from_low, from_high = z > 0, z < last

        @pl.loop(0, cb // BLOCK)
        def _(step):
            here = pl.ds(pl.multiple_of(step * BLOCK, BLOCK), BLOCK)
            own = pl.ds(pl.multiple_of(z * cb + step * BLOCK, BLOCK), BLOCK)
            total = es[k][own, :]
            total = total + jnp.where(from_low, ru[k][own, :], 0.0)
            ge[here, turn_cols(k)] = total + jnp.where(from_high, rd[k][own, :], 0.0)

    def probs_gradient(k):
        at = three_turn_cols(k)

        @pl.loop(0, PLANE * rows // TALL)
        def _(step):
            tall = pl.ds(pl.multiple_of(step * TALL, TALL), TALL)
            part = product(grad_3[tall, at], expr_3[:, at], ((1,), (1,)))
            if k == 0:
                fs[tall, :] = part
            else:
                fs[tall, :] += part

    def slide_of(p, m):
        return pl.ds(pl.multiple_of(p * rows + m * slide_rows, slide_rows), slide_rows)

    def sum_probs_cores():
        for p in mates + (q,):
            fx[p] = fs[slide_of(p, 1 - core), :]
            send(fx.at[p], fy.at[p], fx_s, fx_r.at[p], sibling)

    def return_probs():
        for p in mates:
            arrived(fy.at[p], fx_r.at[p])
            fz[p] = fs[slide_of(p, core), :] + fy[p]
            send(fz.at[p], fr.at[q], f_s, f_r.at[q], mate(p))
        arrived(fy.at[q], fx_r.at[q])
        fr[q] = fs[slide_of(q, core), :] + fy[q]

    def pass_terms():
        for p in mates:
            arrived(l1.at[p], l1_r.at[p])
        l2[z] = (l1[0] + l1[1]) + (l1[2] + l1[3])
        for o in others:
            send(l2.at[z], l2.at[z], l2_s, l2_r.at[z], (o * PLANE + q, core))

    def part_of(slide, m):
        start = slide * slide_rows + m * (slide_rows // 2)
        return pl.ds(pl.multiple_of(start, slide_rows // 2), slide_rows // 2)

    def finish_logits():
        arrived(inn.at[1 - core], in_r)
        rowv[2] = (inn[0] + inn[1]) + rowv[1] * rowv[0]
        for p in mates:
            arrived(fr.at[p], f_r.at[p])
        for m in range(2):

            @pl.loop(0, slide_rows // STEP_ROWS // 2)
            def _(step):
                row_at = (m * (slide_rows // STEP_ROWS // 2) + step) * STEP_ROWS
                at = pl.ds(pl.multiple_of(row_at, STEP_ROWS), STEP_ROWS)
                whole_at = pl.ds(pl.multiple_of(core * slide_rows + row_at, STEP_ROWS), STEP_ROWS)
                by_mass, total_inner = rowv[1, whole_at, 0:1], rowv[2, whole_at, 0:1]
                for p in range(PLANE):
                    for line in range(lines):
                        here, there = pl.ds(line * cb, cb), (line * PLANE + p) * cb
                        grad = fr[p, at, here] + by_mass * weights[:, there : there + cb]
                        glog[whole_at, pl.ds(there, cb)] = pq[p, whole_at, here] * (grad - total_inner)

            here = part_of(core, m)
            send(glog.at[here], glog.at[here], go_s, go_r.at[m], sibling)

    def forward_left():
        for k in range(chunks):

            @pl.when(z < last)
            def _():
                sent(bb[k].at[block(z)], ou_s.at[k])

            @pl.when(z > 0)
            def _():
                sent(bb[k].at[block(z)], od_s.at[k])

            for at in range(1, last):

                @pl.when(z == at)
                def _():
                    sent(bb[k].at[pl.ds(0, at * cb)], fu_s.at[k])
                    sent(bb[k].at[pl.ds((at + 1) * cb, (last - at) * cb)], fd_s.at[k])

        three = pl.ds(0, len(mates))
        sent(ab.at[three, half(0)], a_s)
        sent(ab.at[three, half(0)], a2_s)
        sent(rs.at[three], r_s)
        sent(t0.at[three], t0_s)
        sent(p0.at[three], p0_s)
        for k in range(chunks):
            sent(cr[k].at[three], c_s.at[k])
        sent(s1.at[three], s1_s)
        sent(s2.at[pl.ds(0, last)], s2_s)
        sent(ss.at[0], ss_s)

    steps = {
        "far": forward_far,
        "near": forward_near,
        "share": share_logits,
        "take": take_probs,
        "whole": gathered,
        "product": forward_product,
        "sum": finish_pred,
        "turn": transpose,
        "plane": sum_plane,
        "line": sum_line,
        "genes": finish_genes,
        "cores": sum_cores,
        "spots": finish_spots,
        "grad": send_grad,
        "terms": send_terms,
        "backward": backward_product,
        "probs": probs_gradient,
        "exchange": sum_probs_cores,
        "return": return_probs,
        "loss": pass_terms,
        "logits": finish_logits,
        "add_near": add_near,
        "add_far": add_far,
        "expr": finish_expr,
        "left": forward_left,
    }
    for name, *where in STEPS:
        steps[name](*where)

    for o in others:
        arrived(l2.at[o], l2_r.at[o])
    loss = l2[0]
    for line in range(1, lines):
        loss = loss + l2[line]
    loss_ref[...] = loss[0:1, 0:1] - (inn[0, 0:1, 1:2] + inn[1, 0:1, 1:2])
    for m in range(2):
        arrived(glog.at[part_of(1 - core, m)], go_r.at[m])

    for k in range(turns):
        for at in range(lines):

            @pl.when(z == at)
            def _():
                if at < last:
                    sent(es[k].at[pl.ds((at + 1) * cb, (last - at) * cb)], ru_s.at[k])
                if at > 0:
                    sent(es[k].at[pl.ds(0, at * cb)], rd_s.at[k])

    three = pl.ds(0, len(mates))
    for k in range(1, turns):
        sent(ds[k].at[pl.ds(0, len(mates) * rows)], d_s.at[k])
    sent(vr.at[three], vr_s)
    sent(inn.at[0], in_s)
    sent(l1.at[three], l1_s)
    sent(l2.at[pl.ds(0, last)], l2_s)
    sent(fr.at[three], f_s)
    sent(fx, fx_s)
    sent(glog.at[half(0)], go_s)


def lane_groups(value):
    parts = [value[:, at : at + LANES] for at in range(0, value.shape[1], LANES)]
    return functools.reduce(lambda a, b: a + b, parts)


def grouped(refs, sizes):
    at = 0
    for size in sizes:
        yield refs[at : at + size]
        at += size


def deliver(pred_in, loss_in, glog_in, gexp_in, pred_ref, loss_ref, glog_ref, gexp_ref, sems):
    slides, slide_rows = pred_ref.shape[0], pred_ref.shape[1]
    pairs = [(gexp_in, gexp_ref), (loss_in, loss_ref)]
    for m in range(slides):
        part = pl.ds(m * slide_rows, slide_rows)
        pairs += [(glog_in.at[part], glog_ref.at[m]), (pred_in.at[part], pred_ref.at[m])]
    copies = [pltpu.make_async_copy(src, dst, sems.at[at]) for at, (src, dst) in enumerate(pairs)]
    for copy in copies:
        copy.start()
    for copy in copies:
        copy.wait()


def plane_call(logits, expr, spatial, slide_spots, spot_cells, cell_prior, lines):
    slides, slide_rows, cells = logits.shape
    rows = slides * slide_rows
    cb, genes = expr.shape
    quarter = lines * cb
    spots = PLANE * rows
    chunks, turns = len(FORWARD), len(BACKWARD)
    dma = pltpu.SemaphoreType.DMA
    vmem = pltpu.VMEM
    anywhere = pl.BlockSpec(memory_space=pl.ANY)
    in_vmem = pl.BlockSpec(memory_space=pltpu.VMEM)
    scratch = [
        pltpu.SMEM((slides,), jnp.int32),
        vmem((slides, slide_rows), jnp.int32),
        vmem((1, cells), jnp.int32),
        vmem((rows, cells), F32),
        vmem((PLANE, slide_rows, quarter), F32),
        vmem((rows, genes), F32),
        vmem((cb, genes), F32),
        vmem((PLANE, rows, quarter), F32),
        vmem((PLANE, rows, quarter), F32),
        vmem((PLANE, rows, quarter), F32),
        vmem((spots, 3 * quarter), BF16),
        vmem((quarter, 3 * spots), BF16),
        vmem((quarter, 3 * genes), BF16),
        vmem((3, rows, LANES), F32),
        vmem((PLANE, 8, genes), F32),
        vmem((lines, 8, genes), F32),
        vmem((8, genes), F32),
        vmem((2, 8, rows), F32),
        vmem((3, rows, LANES), F32),
        vmem((PLANE, 8, rows), F32),
        vmem((spots, 3 * genes), BF16),
        vmem((3 * max(quarter, spots), max(FORWARD + BACKWARD)), BF16),
        vmem((PLANE, rows, BACKWARD[0]), F32),
        vmem((PLANE, rows, BACKWARD[0]), F32),
        vmem((PLANE, 8, rows), F32),
        vmem((spots, quarter), F32),
        vmem((PLANE, slide_rows, quarter), F32),
        vmem((PLANE, slide_rows, quarter), F32),
        vmem((PLANE, slide_rows, quarter), F32),
        vmem((PLANE, slide_rows, quarter), F32),
        vmem((2, rows, LANES), F32),
        vmem((PLANE, 8, LANES), F32),
        vmem((lines, 8, LANES), F32),
        dma((2 * slides + 4,)),
        dma((chunks,)),
        dma((chunks,)),
        dma((chunks,)),
        dma((chunks,)),
        dma((chunks,)),
        dma((chunks,)),
        dma((chunks,)),
        dma((chunks,)),
        dma,
        dma((PLANE,)),
        dma,
        dma((PLANE,)),
        dma,
        dma((PLANE,)),
        dma((chunks,)),
        dma((chunks, PLANE)),
        dma,
        dma((2, PLANE)),
        dma,
        dma((2, lines)),
        dma,
        dma,
        dma((turns,)),
        dma((turns, PLANE)),
        dma((turns,)),
        dma((turns, lines)),
        dma((turns,)),
        dma((turns, lines)),
        dma,
        dma((PLANE,)),
        dma,
        dma((PLANE,)),
        dma,
        dma((2,)),
        dma,
        dma,
        dma,
        dma((PLANE,)),
        dma,
        dma((lines,)),
        dma,
        dma((PLANE,)),
        dma,
        dma((PLANE,)),
        dma,
        dma((PLANE,)),
    ]
    for shape, widths in (
        ((quarter,), FORWARD),
        ((spots,), FORWARD),
        ((PLANE, rows), FORWARD),
        ((spots,), BACKWARD),
        ((quarter,), BACKWARD),
        ((quarter,), BACKWARD),
        ((quarter,), BACKWARD),
    ):
        scratch += [vmem(shape + (width,), F32) for width in widths]
    in_hbm = functools.partial(pltpu.with_memory_space_constraint, memory_space=pltpu.HBM)
    in_place = functools.partial(pltpu.with_memory_space_constraint, memory_space=pltpu.VMEM)
    results = pl.pallas_call(
        functools.partial(plane_kernel, lines, FORWARD, BACKWARD),
        out_shape=(
            vmem((rows, genes), F32),
            vmem((1, 1), F32),
            vmem((rows, cells), F32),
            vmem((cb, genes), F32),
        ),
        in_specs=[anywhere] * 6,
        out_specs=(in_vmem,) * 4,
        scratch_shapes=scratch,
        compiler_params=pltpu.CompilerParams(
            collective_id=0, has_side_effects=True, vmem_limit_bytes=48 * 1024 * 1024
        ),
    )(*map(in_hbm, (logits, expr, spatial, slide_spots, spot_cells, cell_prior.reshape(1, cells))))
    pred, loss, grad_logits, grad_expr = pl.pallas_call(
        deliver,
        out_shape=(
            jax.ShapeDtypeStruct((slides, slide_rows, genes), F32),
            jax.ShapeDtypeStruct((1, 1), F32),
            jax.ShapeDtypeStruct((slides, slide_rows, cells), F32),
            jax.ShapeDtypeStruct((cb, genes), F32),
        ),
        in_specs=[anywhere] * 4,
        out_specs=(anywhere,) * 4,
        scratch_shapes=[dma((2 * slides + 2,))],
        compiler_params=pltpu.CompilerParams(vmem_limit_bytes=4 * 1024 * 1024),
    )(*map(in_place, results))
    return pred, loss.reshape(()), grad_logits, grad_expr


def general_plan(logits, expr, spatial, slide_spots, spot_cells, cell_prior):
    place = lax.axis_index("spot")
    side = lax.axis_index("gene")
    rows_all = logits.shape[1]
    cell_rows = expr.shape[0]
    weights = cell_prior.astype(jnp.float32) / fixed_point
    gene_share = (place == 0).astype(jnp.float32)
    row_share = (side == 0).astype(jnp.float32)
    own_weights = lax.dynamic_slice_in_dim(weights, place * cell_rows, cell_rows, 0)
    expr_acc = jnp.zeros((cell_rows, expr.shape[1]), jnp.float32)
    loss_local = jnp.zeros((), jnp.float32)
    pred_list = []
    grad_list = []
    for slide in range(logits.shape[0]):
        logit_rows = logits[slide]
        counted = spot_cells[slide].astype(jnp.float32)
        target = spatial[slide]
        positions = place * rows_all + jnp.arange(rows_all, dtype=jnp.int32)
        valid = (positions < slide_spots[slide]).astype(jnp.float32)
        peak = jnp.max(logit_rows, axis=1, keepdims=True)
        raised = jnp.exp(logit_rows - peak)
        probs = raised / jnp.sum(raised, axis=1, keepdims=True)
        mass = jnp.dot(probs, weights, precision=lax.Precision.HIGHEST)
        blocks = lax.all_to_all(probs, "spot", split_axis=1, concat_axis=0, tiled=True)
        pred = lax.psum_scatter(
            jnp.dot(blocks, expr, precision=lax.Precision.HIGHEST),
            "spot",
            scatter_dimension=0,
            tiled=True,
        )
        gene_dot = jnp.sum(valid[:, None] * pred * target, axis=0)
        gene_pred = jnp.sum(valid[:, None] * pred * pred, axis=0)
        gene_true = jnp.sum(valid[:, None] * target * target, axis=0)
        mass_part = jnp.sum(valid * mass)
        kcell = valid * counted
        cell_part = jnp.sum(kcell)
        spot_dot = jnp.sum(pred * target, axis=1)
        spot_pred = jnp.sum(pred * pred, axis=1)
        spot_true = jnp.sum(target * target, axis=1)
        gene_dot, gene_pred, gene_true, mass_total, cell_total = lax.psum(
            (gene_dot, gene_pred, gene_true, mass_part, cell_part), "spot"
        )
        spot_dot, spot_pred, spot_true = lax.psum((spot_dot, spot_pred, spot_true), "gene")
        gene_inv = lax.rsqrt(gene_pred * gene_true + tiny)
        cos_gene = gene_dot * gene_inv
        spot_inv = lax.rsqrt(spot_pred * spot_true + tiny)
        cos_spot = spot_dot * spot_inv
        share = kcell / cell_total
        scale_count = slide_spots[slide].astype(jnp.float32)
        kl_part = jnp.sum(
            share * (jnp.log(counted) - jnp.log(cell_total) - jnp.log(mass) + jnp.log(mass_total))
        )
        loss_local = loss_local - gene_share * jnp.sum(cos_gene)
        loss_local = loss_local + row_share * (scale_count * kl_part - jnp.sum(valid * cos_spot))
        gene_back = cos_gene * gene_true / (gene_pred * gene_true + tiny)
        spot_back = cos_spot * spot_true / (spot_pred * spot_true + tiny)
        dpred = -valid[:, None] * (
            target * (gene_inv[None, :] + spot_inv[:, None])
            - pred * gene_back[None, :]
            - pred * spot_back[:, None]
        )
        dmass = scale_count * valid * (1.0 / mass_total - share / mass)
        pred_list.append(pred)
        grads_full, mass_full = (
            lax.all_gather(dpred, "spot", axis=0, tiled=True),
            lax.all_gather(dmass, "spot", axis=0, tiled=True),
        )
        dprob_cells = jnp.dot(grads_full, expr.T, precision=lax.Precision.HIGHEST)
        dprob_cells = lax.psum(dprob_cells, "gene")
        expr_acc = expr_acc + lax.dot_general(
            blocks, grads_full, (((0,), (0,)), ((), ())), precision=lax.Precision.HIGHEST
        )
        dprob_cells = dprob_cells + mass_full[:, None] * own_weights[None, :]
        dprob_rows = lax.all_to_all(dprob_cells, "spot", split_axis=0, concat_axis=1, tiled=True)
        inner = jnp.sum(probs * dprob_rows, axis=1, keepdims=True)
        dlogit = probs * (dprob_rows - inner)
        grad_list.append(dlogit)
    loss = lax.psum(loss_local, ("spot", "gene"))
    return (jnp.stack(pred_list), loss, jnp.stack(grad_list), expr_acc)


def solution(mesh):
    places = mesh.shape["spot"]

    def on_device(logits, expr, spatial, slide_spots, spot_cells, cell_prior):
        if places == PLANE * PLANE and mesh.shape["gene"] == 2 and expr.shape[1] == sum(FORWARD):
            return plane_call(
                logits, expr, spatial, slide_spots, spot_cells, cell_prior, places // PLANE
            )
        return general_plan(logits, expr, spatial, slide_spots, spot_cells, cell_prior)

    in_specs = (
        P(None, "spot", None),
        P("spot", "gene"),
        P(None, "spot", "gene"),
        P(),
        P(None, "spot"),
        P(),
    )
    out_specs = (P(None, "spot", "gene"), P(), P(None, "spot", None), P("spot", "gene"))
    return jax.shard_map(
        on_device, mesh=mesh, in_specs=in_specs, out_specs=out_specs, check_vma=False
    )
```

profile of v0, /device:TPU:0, one launch (start us, length us, event | category | flops | bytes accessed | tf_op | source)
XLA Modules:
  0.0 101.0 jit_solution(13222870269789948892)
XLA Ops:
  0.6 98.3 %shard_map.93 = (f32[128,1024]{1,0:T(8,128)S(1)}, f32[1,1]{1,0:T(1,128)}, f32[128,2048]{1,0:T(8,128)S(1)}, f32[128,1024]{1,0:T(8,128)S(1)}) custom-call(f32[2,64,2048]{2,1,0:T(8,128)} %refs_0_.1, f32[128,1024]{1,0:T(8,128)} %refs_1_.1, f32[2,64,1024]{2,1,0:T(8,128)} %refs_2_.1, s32[2]{0:T(128)} %refs_3_.1, s32[2,64]{1,0:T(2,128)} %refs_4_.1, s32[1,2048]{1,0:T(1,128)} %bitcast.2), custom_call_target="tpu_custom_call" | custom-call | tf_op jit(solution)/shard_map/pallas_call | solution.py:983
  99.0 2.0 %shard_map.94 = (f32[2,64,1024]{2,1,0:T(8,128)}, f32[1,1]{1,0:T(1,128)}, f32[2,64,2048]{2,1,0:T(8,128)}, f32[128,1024]{1,0:T(8,128)}) custom-call(f32[128,1024]{1,0:T(8,128)S(1)} %get-tuple-element.12.pred_in, f32[1,1]{1,0:T(1,128)} %get-tuple-element.13.loss_in, f32[128,2048]{1,0:T(8,128)S(1)} %get-tuple-element.14.glog_in, ...), custom_call_target="tpu_custom_call" | custom-call | tf_op jit(solution)/shard_map/pallas_call | solution.py:998
where the time goes:
time: 101 us
  Pallas kernels  100 us (99%)
    pallas_call x1, Pallas kernels, plane_call(): pl.pallas_call(functools.partial(plane_kernel, lines, FORWARD, BACKWARD),...  98.3 us

commit v1 on v0

--- a/solution.py
+++ b/solution.py
@@ -22,7 +22,7 @@
 BACKWARD = (128, 128, 256, 256, 256)
 SPLIT = 4
 LEAD = 1
-NEAR_LEAD = 3
+NEAR_LEAD = 2
 EARLY = 3
 STEPS = (
     ("far", 0),

time: 101 us -> 101 us (level)
  no operation moved by 1% of the time
where the time goes in v1:
time: 101 us
  Pallas kernels  100 us (99%)
    pallas_call x1, Pallas kernels, plane_call(): pl.pallas_call(functools.partial(plane_kernel, lines, FORWARD, BACKWARD),...  98.1 us

profile of v1, /device:TPU:0, one launch (start us, length us, event | category | flops | bytes accessed | tf_op | source)
XLA Modules:
  0.0 100.7 jit_solution(8448183474739371171)
XLA Ops:
  0.6 98.1 %shard_map.93 = (f32[128,1024]{1,0:T(8,128)S(1)}, f32[1,1]{1,0:T(1,128)}, f32[128,2048]{1,0:T(8,128)S(1)}, f32[128,1024]{1,0:T(8,128)S(1)}) custom-call(f32[2,64,2048]{2,1,0:T(8,128)} %refs_0_.1, f32[128,1024]{1,0:T(8,128)} %refs_1_.1, f32[2,64,1024]{2,1,0:T(8,128)} %refs_2_.1, s32[2]{0:T(128)} %refs_3_.1, s32[2,64]{1,0:T(2,128)} %refs_4_.1, s32[1,2048]{1,0:T(1,128)} %bitcast.2), custom_call_target="tpu_custom_call" | custom-call | tf_op jit(solution)/shard_map/pallas_call | solution.py:983
  98.7 2.0 %shard_map.94 = (f32[2,64,1024]{2,1,0:T(8,128)}, f32[1,1]{1,0:T(1,128)}, f32[2,64,2048]{2,1,0:T(8,128)}, f32[128,1024]{1,0:T(8,128)}) custom-call(f32[128,1024]{1,0:T(8,128)S(1)} %get-tuple-element.12.pred_in, f32[1,1]{1,0:T(1,128)} %get-tuple-element.13.loss_in, f32[128,2048]{1,0:T(8,128)S(1)} %get-tuple-element.14.glog_in, ...), custom_call_target="tpu_custom_call" | custom-call | tf_op jit(solution)/shard_map/pallas_call | solution.py:998

commit v2 on v1

--- a/solution.py
+++ b/solution.py
@@ -577,7 +577,8 @@
             @pl.when(z == 0)
             def _():
                 if halved(k):
-                    pass_up(k, middle if turn == 0 else 1, middle if turn == 0 else middle - 1, turn)
+                    for line in range(last, middle - 1, -1) if turn == 0 else range(middle - 1, 0, -1):
+                        pass_up(k, line, 1, line)
                 elif whole(k):
                     if turn == 0:
                         pass_up(k, 1, last, 0)
@@ -588,7 +589,8 @@
             @pl.when(z == last)
             def _():
                 if halved(k):
-                    pass_down(k, 0 if turn == 0 else middle, middle if turn == 0 else middle - 1, turn)
+                    for line in range(middle) if turn == 0 else range(middle, last):
+                        pass_down(k, line, 1, line)
                 elif whole(k):
                     if turn == 0:
                         pass_down(k, 0, last, 0)
@@ -629,8 +631,8 @@
         in_blocks(line * cb, count * cb, add)
 
     def rising(k, at):
-        if halved(k) or whole(k):
-            start = middle if halved(k) else at
+        if whole(k):
+            start = at
             take_up(k, start, lines - start, 0)
             above = max(at + 1, start)
             add_up(k, above, lines - above)
@@ -642,8 +644,8 @@
                 pass_up(k, line, 1, line)
 
     def falling(k, at):
-        if halved(k) or whole(k):
-            end = middle if halved(k) else at + 1
+        if whole(k):
+            end = at + 1
             take_down(k, 0, end, 0)
             below = min(at, end)
             add_down(k, 0, below)
@@ -674,18 +676,14 @@
             @pl.when(z == at)
             def _():
                 if at > 0:
-                    if halved(k) and at < middle:
-                        take_up(k, at, 1, 1)
-                    elif at == last and (halved(k) or whole(k)):
+                    if at == last and whole(k):
                         take_up(k, at, 1, 0)
-                    elif not halved(k) and not whole(k):
+                    elif not whole(k):
                         take_up(k, at, 1, at)
                 if at < last:
-                    if halved(k) and at >= middle:
-                        take_down(k, at, 1, 1)
-                    elif at == 0 and (halved(k) or whole(k)):
+                    if at == 0 and whole(k):
                         take_down(k, at, 1, 0)
-                    elif not halved(k) and not whole(k):
+                    elif not whole(k):
                         take_down(k, at, 1, at)
 
         from_low, from_high = z > 0, z < last

time: 101 us -> 101 us (level)
  no operation moved by 1% of the time
where the time goes in v2:
time: 101 us
  Pallas kernels  100 us (99%)
    pallas_call x1, Pallas kernels, plane_call(): pl.pallas_call(functools.partial(plane_kernel, lines, FORWARD, BACKWARD),...  98.1 us

profile of v2, /device:TPU:0, one launch (start us, length us, event | category | flops | bytes accessed | tf_op | source)
XLA Modules:
  0.0 100.7 jit_solution(14706703613006557420)
XLA Ops:
  0.6 98.1 %shard_map.93 = (f32[128,1024]{1,0:T(8,128)S(1)}, f32[1,1]{1,0:T(1,128)}, f32[128,2048]{1,0:T(8,128)S(1)}, f32[128,1024]{1,0:T(8,128)S(1)}) custom-call(f32[2,64,2048]{2,1,0:T(8,128)} %refs_0_.1, f32[128,1024]{1,0:T(8,128)} %refs_1_.1, f32[2,64,1024]{2,1,0:T(8,128)} %refs_2_.1, s32[2]{0:T(128)} %refs_3_.1, s32[2,64]{1,0:T(2,128)} %refs_4_.1, s32[1,2048]{1,0:T(1,128)} %bitcast.2), custom_call_target="tpu_custom_call" | custom-call | tf_op jit(solution)/shard_map/pallas_call | solution.py:981
  98.7 2.0 %shard_map.94 = (f32[2,64,1024]{2,1,0:T(8,128)}, f32[1,1]{1,0:T(1,128)}, f32[2,64,2048]{2,1,0:T(8,128)}, f32[128,1024]{1,0:T(8,128)}) custom-call(f32[128,1024]{1,0:T(8,128)S(1)} %get-tuple-element.12.pred_in, f32[1,1]{1,0:T(1,128)} %get-tuple-element.13.loss_in, f32[128,2048]{1,0:T(8,128)S(1)} %get-tuple-element.14.glog_in, ...), custom_call_target="tpu_custom_call" | custom-call | tf_op jit(solution)/shard_map/pallas_call | solution.py:996

commit v3 on v2

--- a/solution.py
+++ b/solution.py
@@ -61,8 +61,8 @@
     ("line", 0),
     ("sum", 4),
     ("sum", 5),
+    ("cores",),
     ("plane", 1),
-    ("cores",),
     ("genes", 0),
     ("spots",),
     ("grad", 0),

time: 101 us -> 101 us (level)
  no operation moved by 1% of the time
where the time goes in v3:
time: 101 us
  Pallas kernels  99.9 us (99%)
    pallas_call x1, Pallas kernels, plane_call(): pl.pallas_call(functools.partial(plane_kernel, lines, FORWARD, BACKWARD),...  97.9 us

profile of v3, /device:TPU:0, one launch (start us, length us, event | category | flops | bytes accessed | tf_op | source)
XLA Modules:
  0.0 100.6 jit_solution(10159230804345538742)
XLA Ops:
  0.6 97.9 %shard_map.93 = (f32[128,1024]{1,0:T(8,128)S(1)}, f32[1,1]{1,0:T(1,128)}, f32[128,2048]{1,0:T(8,128)S(1)}, f32[128,1024]{1,0:T(8,128)S(1)}) custom-call(f32[2,64,2048]{2,1,0:T(8,128)} %refs_0_.1, f32[128,1024]{1,0:T(8,128)} %refs_1_.1, f32[2,64,1024]{2,1,0:T(8,128)} %refs_2_.1, s32[2]{0:T(128)} %refs_3_.1, s32[2,64]{1,0:T(2,128)} %refs_4_.1, s32[1,2048]{1,0:T(1,128)} %bitcast.2), custom_call_target="tpu_custom_call" | custom-call | tf_op jit(solution)/shard_map/pallas_call | solution.py:981
  98.6 2.0 %shard_map.94 = (f32[2,64,1024]{2,1,0:T(8,128)}, f32[1,1]{1,0:T(1,128)}, f32[2,64,2048]{2,1,0:T(8,128)}, f32[128,1024]{1,0:T(8,128)}) custom-call(f32[128,1024]{1,0:T(8,128)S(1)} %get-tuple-element.12.pred_in, f32[1,1]{1,0:T(1,128)} %get-tuple-element.13.loss_in, f32[128,2048]{1,0:T(8,128)S(1)} %get-tuple-element.14.glog_in, ...), custom_call_target="tpu_custom_call" | custom-call | tf_op jit(solution)/shard_map/pallas_call | solution.py:996
